TPU v7x, 128 devices: a whole 4x4x4 slice. The times are simulated.
128 devices in a mesh: wide: 16 (over y, x), narrow: 8 (over z, core).
Axes of the slice: x: 4, y: 4, z: 4, core: 2. Of those that a mesh axis runs over, the one named last changes fastest.
Arguments:
- amplitudes: bfloat16 [8, 2048, 2048], P(None, ('wide', 'narrow')), may hold values from -6 to 6
- df_factor: bfloat16 [8, 2048, 2048], P(None, 'wide', 'narrow'), may hold values from -0.0625 to 0.0625
- amp_mask: int32 [16, 16], replicated, may hold values 0 or 1
- factor_mask: int32 [16, 16], replicated, may hold values 0 or 1
Outputs:
- ladder: float32 [8, 2048, 2048], P(None, 'wide', 'narrow')
All inputs are finite; a program needn't handle non-finite values.
Results may differ from a plain program's by a relative error of at most 0.0029.
Values may be sent and summed in bfloat16 or wider, within the bound.
A program may use at most 128 MiB of HBM per device.

v0:
```python
import jax
import jax.numpy as jnp
from jax import lax
from jax.sharding import PartitionSpec as P

V = 2048


def tile_table(mask, row_start, row_count, col_start, col_count):
    tiles = mask.shape[0]
    width = V // tiles
    row_ids = (row_start + jnp.arange(row_count, dtype=jnp.int32)) // width
    col_ids = (col_start + jnp.arange(col_count, dtype=jnp.int32)) // width
    labels = jnp.arange(tiles, dtype=jnp.int32)
    row_hot = (row_ids[:, None] == labels[None, :]).astype(jnp.float32)
    col_hot = (col_ids[:, None] == labels[None, :]).astype(jnp.float32)
    inner = jnp.dot(row_hot, mask.astype(jnp.float32), precision=lax.Precision.HIGHEST)
    return jnp.dot(inner, col_hot.T, precision=lax.Precision.HIGHEST)


def shards(amplitudes, df_factor, amp_mask, factor_mask):
    wide_count = lax.axis_size("wide")
    narrow_count = lax.axis_size("narrow")
    wide_index = lax.axis_index("wide")
    narrow_index = lax.axis_index("narrow")
    pairs, row_block, total = amplitudes.shape
    col_width = total // narrow_count
    a_rows = df_factor.shape[1]
    collected = lax.all_gather(amplitudes, "wide", axis=1, tiled=True)
    split = lax.all_to_all(collected, "narrow", split_axis=2, concat_axis=1, tiled=True)
    split = split.reshape(pairs, narrow_count, wide_count, row_block, col_width)
    relaid = jnp.transpose(split, (0, 2, 1, 3, 4)).reshape(pairs, total, col_width)
    d_start = narrow_index * col_width
    amp_table = tile_table(amp_mask, 0, total, d_start, col_width)
    amps = relaid * amp_table.astype(jnp.bfloat16)[None]
    a_start = wide_index * a_rows
    factor_table = tile_table(factor_mask, a_start, a_rows, d_start, col_width)
    factor = df_factor * factor_table.astype(jnp.bfloat16)[None]
    factor_rows_all = lax.all_gather(factor, "narrow", axis=2, tiled=True)
    halfway = jnp.einsum("pac,icd->ipad", factor_rows_all, amps, preferred_element_type=jnp.float32)
    halfway = halfway.astype(jnp.bfloat16)
    partial_sums = jnp.einsum(
        "ipad,pbd->iab",
        halfway,
        lax.all_gather(factor, "wide", axis=1, tiled=True),
        preferred_element_type=jnp.float32,
    )
    return lax.psum_scatter(partial_sums, "narrow", scatter_dimension=2, tiled=True)


def solution(mesh):
    return jax.shard_map(
        shards,
        mesh=mesh,
        in_specs=(P(None, ("wide", "narrow"), None), P(None, "wide", "narrow"), P(), P()),
        out_specs=P(None, "wide", "narrow"),
        check_vma=False,
    )
```

profile of v0, /device:TPU:1, one launch (start us, length us, event | category | flops | bytes accessed | tf_op | source)
XLA Modules:
  0.0 317.7 jit_solution(5454823913577489325)
XLA Ops:
  6.5 0.0 all-gather.4.cloned.1.call-start
  6.5 2.1 copy.13
  8.7 0.0 all-gather.4.cloned.1.call-update
  8.7 0.0 all-gather.6.cloned.1.call-start
  8.8 0.9 fusion.22
  9.7 0.4 convolution_convert_fusion.1
  10.1 1.9 broadcast_multiply_fusion
  12.0 0.0 all-gather.6.cloned.1.call-update
  12.0 0.0 all-gather.8.cloned.1.call-start
  12.0 0.7 all-gather.8.cloned.1.call-update
  12.7 70.6 %all-gather.4.cloned.1.call-done = bf16[8,256,2048]{2,0,1:T(8,128)(2,1)} async-done(((bf16[8,16,2048]{2,0,1:T(8,128)(2,1)}), bf16[8,256,2048]{2,0,1:T(8,128)(2,1)}) %all-gather.4.cloned.1.call-update) | async-done | bytes 8388624 | tf_op jit(solution)/shard_map/all_gather | solution.py:29
  83.4 13.4 %copy.14 = bf16[8,256,2048]{1,0,2:T(8,128)(2,1)} copy(bf16[8,256,2048]{2,0,1:T(8,128)(2,1)} %all-gather.4.cloned.1.call-done) | data formatting | bytes 16777216 | tf_op jit(solution)/shard_map/all_gather | solution.py:29
  96.7 0.0 copy-start
  96.7 5.7 %all-to-all-start = ((bf16[8,256,2048]{1,0,2:T(8,128)(2,1)}), bf16[8,256,2048]{1,0,2:T(8,128)(2,1)}, u32[]{:S(2)}, u32[]{:S(2)}) async-start(bf16[8,256,2048]{1,0,2:T(8,128)(2,1)} %copy.14), calls=%async_computation | async-start | bytes 16777216 | tf_op jit(solution)/shard_map/all_to_all | solution.py:30
  102.5 0.0 reduce-scatter.2.cloned.1.call-start
  102.5 0.0 copy-done
  102.5 1.0 fusion.18
  103.5 1.1 convolution_convert_fusion
  104.5 102.9 %all-to-all-done = bf16[8,256,2048]{1,0,2:T(8,128)(2,1)} async-done(((bf16[8,256,2048]{1,0,2:T(8,128)(2,1)}), bf16[8,256,2048]{1,0,2:T(8,128)(2,1)}, u32[]{:S(2)}, u32[]{:S(2)}) %all-to-all-start) | async-done | bytes 8388640 | tf_op jit(solution)/shard_map/all_to_all | solution.py:30
  207.4 12.6 %copy.16 = bf16[8,8,256,256]{3,2,1,0:T(8,128)(2,1)} copy(bf16[8,8,256,256]{2,0,3,1:T(8,128)(2,1)} %bitcast.2) | data formatting | bytes 16777216 | tf_op jit(solution)/shard_map/all_to_all | solution.py:30
  220.0 7.9 %copy.17 = bf16[8,16,8,16,256]{4,3,2,1,0:T(8,128)(2,1)} copy(bf16[8,16,8,16,256]{4,3,1,2,0:T(8,128)(2,1)} %bitcast.37) | data formatting | bytes 16777216 | tf_op jit(solution)/shard_map/transpose | solution.py:32
  227.9 7.5 %bitcast_multiply_fusion = bf16[8,2048,256]{2,1,0:T(8,128)(2,1)} fusion(bf16[8,16,8,16,256]{4,3,2,1,0:T(8,128)(2,1)} %copy.17, bf16[2048,256]{1,0:T(8,128)(2,1)S(1)} %convolution_convert_fusion), kind=kLoop, calls=%fused_computation.4 | loop fusion | flops 4194304 | bytes 17825792 | tf_op jit(solution)/shard_map/mul | solution.py:35
  235.4 0.0 all-gather.6.cloned.1.call-done
  235.4 0.0 all-gather.8.cloned.1.call-done
  235.4 25.6 %fusion.4 = f32[8,128,2048]{2,1,0:T(8,128)} fusion(bf16[8,2048,256]{2,1,0:T(8,128)(2,1)} %all-gather.8.cloned.1.call-done, bf16[8,2048,256]{2,1,0:T(8,128)(2,1)} %bitcast_multiply_fusion, bf16[8,128,2048]{2,1,0:T(8,128)(2,1)} %all-gather.6.cloned.1.call-done), kind=kOutput, calls=%fused_computation.5 | convolution fusion | flops 17181966336 | bytes 29360128 | tf_op jit(solution)/shard_map/ipad,pbd->iab/dot_general | solution.py:42
  261.0 0.0 reduce-scatter.2.cloned.1.call-update
  261.0 50.1 %reduce-scatter.2.cloned.1.call-done = f32[8,128,256]{2,1,0:T(8,128)} async-done(((f32[8,128,2048]{2,1,0:T(8,128)}), f32[8,128,256]{2,1,0:T(8,128)}) %reduce-scatter.2.cloned.1.call-update) | async-done | bytes 1048592 | tf_op jit(solution)/shard_map/reduce_scatter | solution.py:48
  (3 shorter events, 0.0 us)
Async XLA Ops:
  6.5 76.8 %all-gather.4.cloned.1.call-start = ((), (), s32[]{:S(2)}) async-start(), calls=%async_computation.2 | async-start | bytes 8912896 | tf_op jit(solution)/shard_map/all_gather | solution.py:29
  8.7 226.7 %all-gather.6.cloned.1.call-start = ((), (), s32[]{:S(2)}) async-start(), calls=%async_computation.3 | async-start | bytes 4718592 | tf_op jit(solution)/shard_map/all_gather | solution.py:39
  12.0 223.4 %all-gather.8.cloned.1.call-start = ((), (), s32[]{:S(2)}) async-start(), calls=%async_computation.4 | async-start | bytes 8912896 | tf_op jit(solution)/shard_map/all_gather | solution.py:45
  96.7 5.7 %copy-start = (s32[16,16]{1,0:T(8,128)S(1)}, s32[16,16]{1,0:T(8,128)}, u32[]{:S(2)}) copy-start(s32[16,16]{1,0:T(8,128)} %param.6) | copy-start | bytes 3076
  96.7 110.7 %all-to-all-start = ((bf16[8,256,2048]{1,0,2:T(8,128)(2,1)}), bf16[8,256,2048]{1,0,2:T(8,128)(2,1)}, u32[]{:S(2)}, u32[]{:S(2)}) async-start(bf16[8,256,2048]{1,0,2:T(8,128)(2,1)} %copy.14), calls=%async_computation | async-start | bytes 16777216 | tf_op jit(solution)/shard_map/all_to_all | solution.py:30
  102.5 208.7 %reduce-scatter.2.cloned.1.call-start = ((), (), s32[]{:S(2)}) async-start(), calls=%async_computation.5 | async-start | bytes 9437184 | tf_op jit(solution)/shard_map/reduce_scatter | solution.py:48
Sparse Core Ops, SparseCore 0:
  9.5 73.8 all-gather.3
  85.0 57.4 all-gather.5
  144.6 69.9 all-gather.7
  261.1 49.9 reduce-scatter.1
where the time goes:
time: 319 us; the launch traced here: 318 us
  waiting for transfers between devices  224 us (70%)
  local copies, waits for them, and re-layouts  36 us (11%)
  matrix products  28.9 us (9%)
  between operations  13.2 us (4%)
  other arithmetic  9.36 us (3%)
  starting transfers between devices  5.82 us (2%)
    all_to_all x1, waiting for transfers between devices, shards(): lax.all_to_all(collected, 'narrow', split_axis=2, concat_axis=1, tiled=True)  103 us
    all_gather x1, waiting for transfers between devices, shards(): collected = lax.all_gather(amplitudes, 'wide', axis=1, tiled=True)  70.6 us
    reduce_scatter x1, waiting for transfers between devices, shards(): lax.psum_scatter(partial_sums, 'narrow', scatter_dimension=2, tiled=True)  50.1 us
    dot_general x1, matrix products, shards(): jnp.einsum('ipad,pbd->iab', halfway, lax.all_gather(factor, 'wide', axis=...  25.6 us
    all_gather x1, local copies, waits for them, and re-layouts, shards(): collected = lax.all_gather(amplitudes, 'wide', axis=1, tiled=True)  13.4 us
    all_to_all x1, local copies, waits for them, and re-layouts, shards(): lax.all_to_all(collected, 'narrow', split_axis=2, concat_axis=1, tiled=True)  12.6 us
    transpose x1, local copies, waits for them, and re-layouts, shards(): jnp.transpose(split, (0, 2, 1, 3, 4)).reshape(pairs, total, col_width)  7.9 us
    mul x1, other arithmetic, shards(): amps = relaid * amp_table.astype(jnp.bfloat16)[None]  7.45 us
  transfers between devices with their start and end apart: 5, of which 3 were waited for; matrix products, arithmetic and copies ran while one was open for 15% of the time, Pallas kernels for 0%

commit v1 on v0

v1 whole, which is shorter than its diff:
```python
import functools

import jax
import jax.numpy as jnp
from jax import lax
from jax.experimental import pallas as pl
from jax.experimental.pallas import tpu as pltpu
from jax.sharding import PartitionSpec as P

MESH = pl.DeviceIdType.MESH
BF16 = jnp.bfloat16
F32 = jnp.float32
TRANSPOSED = (((1,), (1,)), ((), ()))

LAG = 2.0
FACTOR_CHUNKS = 8
PAIRS = 8


def kernel(amp_ref, fac_ref, amask, fmask, out_ref, tsrc, fsrc, g2, fr, half, part, ring_in, comb, quad, fin, pin, pp,
           g_recv, g_send, f_recv, f_send, e_send, a_recv, a_send, o_recv, o_send, q_send):
    w, n = lax.axis_index("wide"), lax.axis_index("narrow")
    y, x = w // 4, w % 4
    z, c = n // 2, n % 2
    A, xl = x // 2, x % 2
    D = ((x + 1) // 2) % 2
    up = lambda v, s: lax.rem(v + s + 4, 4)
    x_of = lambda a, d: a * 3 + d * (1 - 2 * a)
    dev = lambda yy, xx, zz, cc: (yy * 4 + xx, zz * 2 + cc)
    z1, z2, z3 = up(z, 1), up(z, 2), up(z, 3)
    y1, y2, y3 = up(y, 1), up(y, 2), up(y, 3)
    z_up, z_down = dev(y, x, z1, c), dev(y, x, z3, c)
    y_up, y_down = dev(y1, x, z, c), dev(y3, x, z, c)
    a_pair = dev(y, x_of(1 - A, D), z, c)
    d_pair = dev(y, x_of(A, 1 - D), z, c)
    sibling = dev(y, x, z, 1 - c)
    on_home_chip = x == 2 * A + c

    def push(src, dst, send, recv, to):
        pltpu.make_async_remote_copy(src_ref=src, dst_ref=dst, send_sem=send, recv_sem=recv, device_id=to, device_id_type=MESH).start()

    def push_or_copy(here, src, dst, send, recv, to):
        @pl.when(here)
        def _():
            pltpu.make_async_copy(src, dst, recv).start()

        @pl.when(jnp.logical_not(here))
        def _():
            push(src, dst, send, recv, to)

    def wait(ref, sem):
        pltpu.make_async_copy(ref, ref, sem).wait()

    def units(count):
        return g2.at[pl.ds(0, count), 0, 0, 0]

    barrier = pltpu.get_barrier_semaphore()
    for dz in range(4):
        for dd in range(2):
            for dc in range(2):
                if dz or dd or dc:
                    xx = x_of(A, D if dd == 0 else 1 - D)
                    cc = c if dc == 0 else 1 - c
                    pl.semaphore_signal(barrier, inc=1, device_id=dev(y, xx, up(z, dz), cc), device_id_type=MESH)
    for to in (y_up, y_down, a_pair):
        pl.semaphore_signal(barrier, inc=1, device_id=to, device_id_type=MESH)

    for h in range(2):
        keep = fmask[w, 2 * n + h].astype(F32)
        cols = pl.ds(h * 128, 128)
        fsrc[:, :, cols] = (fac_ref[:, :, cols].astype(F32) * keep).astype(BF16)
    for h in range(16):
        keep = amask[w, h].astype(F32)
        cols = pl.ds(h * 128, 128)
        tsrc[:, :, cols] = (amp_ref[:, :, cols].astype(F32) * keep).astype(BF16)

    pl.semaphore_wait(barrier, 18)

    ends = []

    for k in range(FACTOR_CHUNKS):
        for d in range(2):
            here = jnp.logical_and(x_of(A, d) == x, xl == c)
            wanted = None if k % 2 == 0 else c == d

            def go(k=k, d=d, here=here):
                push_or_copy(here, fsrc.at[k], fr.at[k, z, c], e_send.at[k, d], f_recv.at[k, 5], dev(y, x_of(A, d), z, xl))

            if wanted is None:
                go()
            else:
                pl.when(wanted)(go)
            sent = jnp.logical_not(here) if wanted is None else jnp.logical_and(wanted, jnp.logical_not(here))
            ends.append(lambda k=k, d=d, sent=sent: pl.when(sent)(lambda: wait(fsrc.at[k], e_send.at[k, d])))

    for dz in range(4):
        for d in range(2):
            zz = up(z, dz)
            here = jnp.logical_and(jnp.logical_and(x_of(A, d) == x, xl == c), dz == 0)
            cols = pl.ds(pl.multiple_of((2 * zz + d) * 256, 256), 256)
            rows = pl.ds(pl.multiple_of((2 * z + c) * 16, 16), 16)
            src = tsrc.at[:, :, cols]
            dst = g2.at[pl.ds(8, 8), y, A, xl, rows]
            if dz == 0:
                push_or_copy(here, src, dst, a_send.at[dz, d], a_recv.at[0], dev(y, x_of(A, d), zz, xl))
                ends.append(lambda src=src, dz=dz, d=d, here=here: pl.when(jnp.logical_not(here))(lambda: wait(src, a_send.at[dz, d])))
            else:
                push(src, dst, a_send.at[dz, d], a_recv.at[0], dev(y, x_of(A, d), zz, xl))
                ends.append(lambda src=src, dz=dz, d=d: wait(src, a_send.at[dz, d]))

    lo, hi = pl.ds(0, 64), pl.ds(64, 64)

    def f1(k):
        if k % 2 == 0:
            wait(fr.at[k, z], f_recv.at[k, 5])
        else:
            wait(fr.at[k, z, D], f_recv.at[k, 5])
        g2[k, y, A, c] = fr[k, z, D]
        own = fr.at[k, z] if k % 2 == 0 else fr.at[k, z, D]
        push(own, own, f_send.at[k], f_recv.at[k, 0], z_up)
        push(own, own, f_send.at[k], f_recv.at[k, 1], z_down)
        if k % 2:
            push(own, own, f_send.at[k], f_recv.at[k, 4], d_pair)

    def f2(k):
        if k % 2 == 0:
            wait(fr.at[k, z3], f_recv.at[k, 0])
            push(fr.at[k, z3, 0], fr.at[k, z3, 0], f_send.at[k], f_recv.at[k, 2], z_up)
            wait(fr.at[k, z1], f_recv.at[k, 1])
            push(fr.at[k, z1, 1], fr.at[k, z1, 1], f_send.at[k], f_recv.at[k, 3], z_down)
        else:
            wait(fr.at[k, z3, D], f_recv.at[k, 0])
            push(fr.at[k, z3, D, lo], fr.at[k, z3, D, lo], f_send.at[k], f_recv.at[k, 2], z_up)
            push(fr.at[k, z3, D], fr.at[k, z3, D], f_send.at[k], f_recv.at[k, 4], d_pair)
            wait(fr.at[k, z1, D], f_recv.at[k, 1])
            push(fr.at[k, z1, D, hi], fr.at[k, z1, D, hi], f_send.at[k], f_recv.at[k, 3], z_down)
            push(fr.at[k, z1, D], fr.at[k, z1, D], f_send.at[k], f_recv.at[k, 4], d_pair)

    def f3(k):
        if k % 2 == 0:
            wait(fr.at[k, z2, 0], f_recv.at[k, 2])
            wait(fr.at[k, z2, 1], f_recv.at[k, 3])
            ends.append(lambda: wait(units(6), f_send.at[k]))
        else:
            wait(fr.at[k, z2, D, lo], f_recv.at[k, 2])
            wait(fr.at[k, z2, D, hi], f_recv.at[k, 3])
            push(fr.at[k, z2, D], fr.at[k, z2, D], f_send.at[k], f_recv.at[k, 4], d_pair)
            ends.append(lambda: wait(units(7), f_send.at[k]))

    def f4(k):
        if k % 2:
            wait(fr.at[k, :, 1 - D], f_recv.at[k, 4])

    def s1(k):
        own = g2.at[k, y, A, c]
        if k == 8:
            wait(g2.at[pl.ds(8, 8), y, A, c], a_recv.at[0])
        if k % 2 == 0:
            push(own, own, g_send.at[k], g_recv.at[k, 4], a_pair)
        else:
            push(own, own, g_send.at[k], g_recv.at[k, 0], y_up)
            push(own, own, g_send.at[k], g_recv.at[k, 1], y_down)
            push(own, own, g_send.at[k], g_recv.at[k, 4], a_pair)

    def s2(k):
        if k % 2 == 0:
            wait(g2.at[k, y, 1 - A, c], g_recv.at[k, 4])
            own = g2.at[k, y, :, c]
            push(own, own, g_send.at[k], g_recv.at[k, 0], y_up)
            push(own, own, g_send.at[k], g_recv.at[k, 1], y_down)
        else:
            b = g2.at[k, y3, A, c]
            wait(b, g_recv.at[k, 0])
            push(b.at[lo], b.at[lo], g_send.at[k], g_recv.at[k, 2], y_up)
            push(b, b, g_send.at[k], g_recv.at[k, 4], a_pair)
            b = g2.at[k, y1, A, c]
            wait(b, g_recv.at[k, 1])
            push(b.at[hi], b.at[hi], g_send.at[k], g_recv.at[k, 3], y_down)
            push(b, b, g_send.at[k], g_recv.at[k, 4], a_pair)

    def s3(k):
        if k % 2 == 0:
            wait(g2.at[k, y3, :, c], g_recv.at[k, 0])
            push(g2.at[k, y3, 0, c], g2.at[k, y3, 0, c], g_send.at[k], g_recv.at[k, 2], y_up)
            wait(g2.at[k, y1, :, c], g_recv.at[k, 1])
            push(g2.at[k, y1, 1, c], g2.at[k, y1, 1, c], g_send.at[k], g_recv.at[k, 3], y_down)
        else:
            b = g2.at[k, y2, A, c]
            wait(b.at[lo], g_recv.at[k, 2])
            wait(b.at[hi], g_recv.at[k, 3])
            push(b, b, g_send.at[k], g_recv.at[k, 4], a_pair)

    def s4(k):
        if k % 2 == 0:
            wait(g2.at[k, y2, 0, c], g_recv.at[k, 2])
            wait(g2.at[k, y2, 1, c], g_recv.at[k, 3])
        else:
            wait(g2.at[k, :, 1 - A, c], g_recv.at[k, 4])
        mine = g2.at[k, :, :, c]
        push(mine, mine, g_send.at[k], g_recv.at[k, 5], sibling)
        ends.append(lambda: wait(units(15), g_send.at[k]))

    def s5(k):
        wait(g2.at[k, :, :, 1 - c], g_recv.at[k, 5])

    def halfway(i):
        for q in range(2):
            acc = jnp.zeros((512, 256), F32)
            for m in range(8):
                rows = fr[pl.ds(4 * q, 4), m // 2, m % 2].reshape(512, 256)
                acc += jnp.dot(rows, g2[8 + i, m // 2, m % 2].reshape(256, 256), preferred_element_type=F32)
            half[pl.ds(4 * q, 4), pl.ds((i % 2) * 128, 128)] = acc.astype(BF16).reshape(4, 128, 256)

    def ladder(j, q):
        acc = jnp.zeros((256, 1024), F32)
        for p in range(8):
            acc += lax.dot_general(half[p], g2[p, pl.ds(2 * q, 2)].reshape(1024, 256), TRANSPOSED, preferred_element_type=F32)
        acc = acc.astype(BF16)
        for h in range(2):
            for m in range(4):
                part[2 * j + h, 2 * q + m // 2, m % 2] = acc[h * 128:(h + 1) * 128, m * 256:(m + 1) * 256]

    add = lambda *terms: functools.reduce(lambda a, b: a + b, [t.astype(F32) for t in terms])

    def owner_push(i, src_of, dst, sem):
        for cc in range(2):
            here = jnp.logical_and(on_home_chip, c == cc)
            src = src_of(cc)
            push_or_copy(here, src, dst, q_send.at[i, cc], sem, dev(y, 2 * A + c, z, cc))
            ends.append(lambda src=src, cc=cc, here=here: pl.when(jnp.logical_not(here))(lambda: wait(src, q_send.at[i, cc])))

    def scatter_first(i, block, first, second):
        send = o_send.at[i]
        rin = ring_in.at[i]
        push(block(z2).at[first], rin.at[0, first], send, o_recv.at[i, 0], z_up)
        push(block(z2, 1).at[second], rin.at[0, second] if i % 2 else rin.at[3, second], send, o_recv.at[i, 1], z_down)
        push(block(z3).at[first], rin.at[1, first], send, o_recv.at[i, 2], z_down)
        push(block(z1, 1).at[second], rin.at[1, second] if i % 2 else rin.at[4, second], send, o_recv.at[i, 3], z_up)

    def o1(i):
        if i % 2 == 0:
            block = lambda zz, d=0: part.at[i, zz, d]
            scatter_first(i, block, pl.ds(0, 128), pl.ds(0, 128))
        else:
            owner_push(i, lambda cc: part.at[i, :, cc], pin.at[i // 2, D], o_recv.at[i, 4])

    def o2(i):
        rin = ring_in.at[i]
        if i % 2 == 0:
            wait(rin.at[0], o_recv.at[i, 0])
            comb[i, 0] = add(part[i, z1, 0], ring_in[i, 0]).astype(BF16)
            push(comb.at[i, 0], rin.at[2], o_send.at[i], o_recv.at[i, 2], z_up)
            wait(rin.at[3], o_recv.at[i, 1])
            comb[i, 1] = add(part[i, z3, 1], ring_in[i, 3]).astype(BF16)
            push(comb.at[i, 1], rin.at[5], o_send.at[i], o_recv.at[i, 3], z_down)
        else:
            j = i // 2
            wait(pin.at[j], o_recv.at[i, 4])
            pp[j] = add(pin[j, 0], pin[j, 1]).astype(BF16)
            scatter_first(i, lambda zz, d=0: pp.at[j, zz], lo, hi)

    def o3(i):
        rin = ring_in.at[i]
        if i % 2 == 0:
            wait(rin.at[pl.ds(1, 2)], o_recv.at[i, 2])
            wait(rin.at[pl.ds(4, 2)], o_recv.at[i, 3])
            quad[i // 2, 0] = add(part[i, z, 0], ring_in[i, 1], ring_in[i, 2]).astype(BF16)
            quad[i // 2, 1] = add(part[i, z, 1], ring_in[i, 4], ring_in[i, 5]).astype(BF16)
            owner_push(i, lambda cc: quad.at[i // 2, cc], fin.at[i // 2, D], o_recv.at[i, 4])
            ends.append(lambda: wait(units(6), o_send.at[i]))
        else:
            j = i // 2
            wait(rin.at[0, lo], o_recv.at[i, 0])
            comb[i, 0, lo] = add(pp[j, z1, lo], ring_in[i, 0, lo]).astype(BF16)
            push(comb.at[i, 0, lo], rin.at[2, lo], o_send.at[i], o_recv.at[i, 2], z_up)
            wait(rin.at[0, hi], o_recv.at[i, 1])
            comb[i, 0, hi] = add(pp[j, z3, hi], ring_in[i, 0, hi]).astype(BF16)
            push(comb.at[i, 0, hi], rin.at[2, hi], o_send.at[i], o_recv.at[i, 3], z_down)
            ends.append(lambda: wait(units(3), o_send.at[i]))

    def o4(i):
        j = i // 2
        if i % 2 == 0:
            wait(fin.at[j], o_recv.at[i, 4])
            out_ref[i] = add(fin[j, 0], fin[j, 1])
        else:
            rin = ring_in.at[i]
            wait(rin.at[pl.ds(1, 2), lo], o_recv.at[i, 2])
            wait(rin.at[pl.ds(1, 2), hi], o_recv.at[i, 3])
            out_ref[i] = add(pin[j, 0, z], pin[j, 1, z], ring_in[i, 1], ring_in[i, 2])

    plan = []

    def at(when, step, *args):
        plan.append((when, len(plan), step, args))

    for k in range(FACTOR_CHUNKS):
        for s, step in enumerate((f1, f2, f3, f4)):
            at(k + s * LAG, step, k)
    for k in range(16):
        for s, step in enumerate((s1, s2, s3, s4, s5)):
            at(k + s * LAG + 0.01, step, k)
    for j in range(PAIRS // 2):
        ready = 8 + 2 * j + 1 + 4 * LAG + 0.02
        at(ready - 1, halfway, 2 * j)
        at(ready, halfway, 2 * j + 1)
        at(ready + 0.3, ladder, j, 0)
        at(ready + 0.6, ladder, j, 1)
        for i in (2 * j + 1, 2 * j):
            for s, step in enumerate((o1, o2, o3, o4)):
                at(ready + 0.7 + 0.6 * s, step, i)
    for _, _, step, args in sorted(plan, key=lambda p: (p[0], p[1])):
        step(*args)
    for end in ends:
        end()


def shards(amplitudes, df_factor, amp_mask, factor_mask):
    vmem, smem = pl.BlockSpec(memory_space=pltpu.VMEM), pl.BlockSpec(memory_space=pltpu.SMEM)
    block = lambda *lead: pltpu.VMEM((*lead, 128, 256), BF16)
    dma = lambda *shape: pltpu.SemaphoreType.DMA(shape)
    return pl.pallas_call(
        kernel,
        out_shape=jax.ShapeDtypeStruct((8, 128, 256), F32),
        in_specs=[vmem, vmem, smem, smem],
        out_specs=vmem,
        scratch_shapes=[
            pltpu.VMEM((8, 16, 2048), BF16),
            block(8),
            block(16, 4, 2, 2),
            block(8, 4, 2),
            pltpu.VMEM((8, 256, 256), BF16),
            block(8, 4, 2),
            block(8, 6),
            block(8, 2),
            block(4, 2),
            block(4, 2),
            block(4, 2, 4),
            block(4, 4),
            dma(16, 6), dma(16), dma(8, 6), dma(8), dma(8, 2), dma(1), dma(4, 2), dma(8, 5), dma(8), dma(8, 2),
        ],
        compiler_params=pltpu.CompilerParams(collective_id=0, has_side_effects=True, vmem_limit_bytes=60 * 2**20),
        cost_estimate=pl.CostEstimate(flops=17179869184, bytes_accessed=4 * 2**20, transcendentals=0),
    )(amplitudes, df_factor, amp_mask, factor_mask)


def solution(mesh):
    return jax.shard_map(
        shards,
        mesh=mesh,
        in_specs=(P(None, ("wide", "narrow"), None), P(None, "wide", "narrow"), P(), P()),
        out_specs=P(None, "wide", "narrow"),
        check_vma=False,
    )
```

time: 319 us -> 139 us (0.44)
  waiting for transfers between devices: 224 us -> 0 us
  Pallas kernels: 0 us -> 137 us
  local copies, waits for them, and re-layouts: 36 us -> 2.27 us
  matrix products: 28.9 us -> 0 us
  between operations: 13.2 us -> 0.01 us
  other arithmetic: 9.36 us -> 0 us
  starting transfers between devices: 5.82 us -> 0 us
    pallas_call x0 -> x1, Pallas kernels: none -> 137 us  [shards(): pl.pallas_call(kernel, out_shape=jax.ShapeDtypeStruct((8, 128, 256), F32)...]
    all_to_all x1 -> x0, waiting for transfers between devices: 103 us -> none  [shards(): lax.all_to_all(collected, 'narrow', split_axis=2, concat_axis=1, tiled=True)]
    all_gather x3 -> x0, waiting for transfers between devices: 70.6 us -> none  [the longest x1 70.6 us: shards(): collected = lax.all_gather(amplitudes, 'wide', axis=1, tiled=True)]
    reduce_scatter x1 -> x0, waiting for transfers between devices: 50.1 us -> none  [shards(): lax.psum_scatter(partial_sums, 'narrow', scatter_dimension=2, tiled=True)]
    dot_general x5 -> x0, matrix products: 28.9 us -> none  [the longest x1 25.6 us: shards(): jnp.einsum('ipad,pbd->iab', halfway, lax.all_gather(factor, 'wide', axis=...]
    all_gather x1 -> x0, local copies, waits for them, and re-layouts: 13.4 us -> none  [shards(): collected = lax.all_gather(amplitudes, 'wide', axis=1, tiled=True)]
    all_to_all x1 -> x0, local copies, waits for them, and re-layouts: 12.6 us -> none  [shards(): lax.all_to_all(collected, 'narrow', split_axis=2, concat_axis=1, tiled=True)]
    mul x2 -> x0, other arithmetic: 9.33 us -> none  [the longest x1 7.45 us: shards(): amps = relaid * amp_table.astype(jnp.bfloat16)[None]]
  transfers between devices with their start and end apart: 5 -> 0, of which waited for: 3 -> 0; matrix products, arithmetic and copies ran while one was open for 15% -> 0% of each run, Pallas kernels for 0% -> 0%
where the time goes in v1:
time: 139 us
  Pallas kernels  137 us (99%)
  local copies, waits for them, and re-layouts  2.27 us (2%)
    pallas_call x1, Pallas kernels, shards(): pl.pallas_call(kernel, out_shape=jax.ShapeDtypeStruct((8, 128, 256), F32)...  137 us

profile of v1, /device:TPU:1, one launch (start us, length us, event | category | flops | bytes accessed | tf_op | source)
XLA Modules:
  0.0 139.0 jit_solution(9518660835265684577)
XLA Ops:
  0.0 136.8 %shard_map.46 = f32[8,128,256]{2,1,0:T(8,128)} custom-call(bf16[8,16,2048]{2,1,0:T(8,128)(2,1)} %amp_ref.1, bf16[8,128,256]{2,1,0:T(8,128)(2,1)} %fac_ref.1, s32[16,16]{1,0:T(8,128)} %amask.1, s32[16,16]{1,0:T(8,128)} %fmask.1), custom_call_target="tpu_custom_call" | custom-call | flops 17179869184 | bytes 4194304 | tf_op jit(solution)/shard_map/pallas_call | solution.py:322
  136.8 2.3 %copy.6 = f32[8,128,256]{2,1,0:T(8,128)} copy(f32[8,128,256]{2,1,0:T(8,128)} %shard_map.46) | data formatting | bytes 2097152

commit v2 on v0

v2 whole, which is shorter than its diff:
```python
import functools
import heapq

import jax
import jax.numpy as jnp
from jax import lax
from jax.experimental import pallas as pl
from jax.experimental.pallas import tpu as pltpu
from jax.sharding import PartitionSpec as P

MESH = pl.DeviceIdType.MESH
BF16 = jnp.bfloat16
F32 = jnp.float32
TRANSPOSED = (((1,), (1,)), ((), ()))

SUB = 2
ROWS = 128 // SUB
FACTOR_LAG = 3.0
AMP_LAG = 3.0
CORE_LAG = 1.0
OUT_LAG = 4.0
AHEAD = 4
SHARE_AT = 2.0
READY = 0.0
END_LAG = 8.0


def kernel(amp_ref, fac_ref, amask, fmask, out_ref, tsrc, fsrc, g2, fr, half, part, part32, ring_in, comb, quad, fin, pin, pp,
           g_recv, g_send, f_recv, f_send, e_send, a_recv, a_send, o_recv, o_send, q_send):
    w, n = lax.axis_index("wide"), lax.axis_index("narrow")
    y, x = w // 4, w % 4
    z, c = n // 2, n % 2
    A, xl = x // 2, x % 2
    D = ((x + 1) // 2) % 2
    up = lambda v, s: lax.rem(v + s + 4, 4)
    x_of = lambda a, d: a * 3 + d * (1 - 2 * a)
    dev = lambda yy, xx, zz, cc: (yy * 4 + xx, zz * 2 + cc)
    z1, z2, z3 = up(z, 1), up(z, 2), up(z, 3)
    y1, y2, y3 = up(y, 1), up(y, 2), up(y, 3)
    z_up, z_down = dev(y, x, z1, c), dev(y, x, z3, c)
    y_up, y_down = dev(y1, x, z, c), dev(y3, x, z, c)
    a_pair = dev(y, x_of(1 - A, D), z, c)
    d_pair = dev(y, x_of(A, 1 - D), z, c)
    sibling = dev(y, x, z, 1 - c)
    on_home_chip = x == 2 * A + c

    def push(src, dst, send, recv, to):
        pltpu.make_async_remote_copy(src_ref=src, dst_ref=dst, send_sem=send, recv_sem=recv, device_id=to, device_id_type=MESH).start()

    def push_or_copy(here, src, dst, send, recv, to):
        @pl.when(here)
        def _():
            pltpu.make_async_copy(src, dst, recv).start()

        @pl.when(jnp.logical_not(here))
        def _():
            push(src, dst, send, recv, to)

    def wait(ref, sem):
        pltpu.make_async_copy(ref, ref, sem).wait()

    def units(count):
        return g2.at[pl.ds(0, count), 0, 0, 0, pl.ds(0, ROWS)]

    def split(q):
        k, first = q // SUB, (q % SUB) * ROWS
        return k, q % 2 == 0 or q % 16 == 15, pl.ds(first, ROWS), pl.ds(first, ROWS // 2), pl.ds(first + ROWS // 2, ROWS // 2)

    barrier = pltpu.get_barrier_semaphore()
    for dz in range(4):
        for dd in range(2):
            for dc in range(2):
                if dz or dd or dc:
                    xx = x_of(A, D if dd == 0 else 1 - D)
                    cc = c if dc == 0 else 1 - c
                    pl.semaphore_signal(barrier, inc=1, device_id=dev(y, xx, up(z, dz), cc), device_id_type=MESH)
    for to in (y_up, y_down, a_pair):
        pl.semaphore_signal(barrier, inc=1, device_id=to, device_id_type=MESH)

    for h in range(2):
        keep = fmask[w, 2 * n + h].astype(F32)
        cols = pl.ds(h * 128, 128)
        fsrc[:, :, cols] = (fac_ref[:, :, cols].astype(F32) * keep).astype(BF16)
    for h in range(16):
        keep = amask[w, h].astype(F32)
        cols = pl.ds(h * 128, 128)
        tsrc[:, :, cols] = (amp_ref[:, :, cols].astype(F32) * keep).astype(BF16)

    pl.semaphore_wait(barrier, 18)

    plan = []
    now = [-100.0, 0]

    def at(when, order, step, *args):
        now[1] += 1
        heapq.heappush(plan, (when, order, now[1], step, args))

    def finish(step):
        at(now[0] + END_LAG, 30, step)

    def e1(q):
        k, pair_first, rows, _, _ = split(q)
        for d in range(2):
            here = jnp.logical_and(x_of(A, d) == x, xl == c)

            def go(d=d, here=here):
                push_or_copy(here, fsrc.at[k, rows], fr.at[k, z, c, rows], e_send.at[q, d], f_recv.at[q, 5], dev(y, x_of(A, d), z, xl))

            if pair_first:
                go()
            else:
                pl.when(c == d)(go)
            sent = jnp.logical_not(here) if pair_first else jnp.logical_and(c == d, jnp.logical_not(here))
            finish(lambda d=d, sent=sent: pl.when(sent)(lambda: wait(fsrc.at[k, rows], e_send.at[q, d])))

    def share_amplitudes():
        for dz in range(4):
            for d in range(2):
                zz = up(z, dz)
                here = jnp.logical_and(jnp.logical_and(x_of(A, d) == x, xl == c), dz == 0)
                cols = pl.ds(pl.multiple_of((2 * zz + d) * 256, 256), 256)
                rows = pl.ds(pl.multiple_of((2 * z + c) * 16, 16), 16)
                src = tsrc.at[:, :, cols]
                dst = g2.at[pl.ds(8, 8), y, A, xl, rows]
                if dz == 0:
                    push_or_copy(here, src, dst, a_send.at[dz, d], a_recv.at[0], dev(y, x_of(A, d), zz, xl))
                    finish(lambda src=src, dz=dz, d=d, here=here: pl.when(jnp.logical_not(here))(lambda: wait(src, a_send.at[dz, d])))
                else:
                    push(src, dst, a_send.at[dz, d], a_recv.at[0], dev(y, x_of(A, d), zz, xl))
                    finish(lambda src=src, dz=dz, d=d: wait(src, a_send.at[dz, d]))

    def f1(q):
        k, pair_first, rows, _, _ = split(q)
        own = fr.at[k, z, :, rows] if pair_first else fr.at[k, z, D, rows]
        wait(own, f_recv.at[q, 5])
        g2[k, y, A, c, rows] = fr[k, z, D, rows]
        push(own, own, f_send.at[q], f_recv.at[q, 0], z_up)
        push(own, own, f_send.at[q], f_recv.at[q, 1], z_down)
        if not pair_first:
            push(own, own, f_send.at[q], f_recv.at[q, 4], d_pair)

    def f2(q):
        k, pair_first, rows, lo, hi = split(q)
        if pair_first:
            wait(fr.at[k, z3, :, rows], f_recv.at[q, 0])
            push(fr.at[k, z3, 0, rows], fr.at[k, z3, 0, rows], f_send.at[q], f_recv.at[q, 2], z_up)
            wait(fr.at[k, z1, :, rows], f_recv.at[q, 1])
            push(fr.at[k, z1, 1, rows], fr.at[k, z1, 1, rows], f_send.at[q], f_recv.at[q, 3], z_down)
        else:
            wait(fr.at[k, z3, D, rows], f_recv.at[q, 0])
            push(fr.at[k, z3, D, lo], fr.at[k, z3, D, lo], f_send.at[q], f_recv.at[q, 2], z_up)
            push(fr.at[k, z3, D, rows], fr.at[k, z3, D, rows], f_send.at[q], f_recv.at[q, 4], d_pair)
            wait(fr.at[k, z1, D, rows], f_recv.at[q, 1])
            push(fr.at[k, z1, D, hi], fr.at[k, z1, D, hi], f_send.at[q], f_recv.at[q, 3], z_down)
            push(fr.at[k, z1, D, rows], fr.at[k, z1, D, rows], f_send.at[q], f_recv.at[q, 4], d_pair)

    def f3(q):
        k, pair_first, rows, lo, hi = split(q)
        if pair_first:
            wait(fr.at[k, z2, 0, rows], f_recv.at[q, 2])
            wait(fr.at[k, z2, 1, rows], f_recv.at[q, 3])
            finish(lambda: wait(units(6), f_send.at[q]))
        else:
            wait(fr.at[k, z2, D, lo], f_recv.at[q, 2])
            wait(fr.at[k, z2, D, hi], f_recv.at[q, 3])
            push(fr.at[k, z2, D, rows], fr.at[k, z2, D, rows], f_send.at[q], f_recv.at[q, 4], d_pair)
            finish(lambda: wait(units(7), f_send.at[q]))

    def f4(q):
        k, pair_first, rows, _, _ = split(q)
        if not pair_first:
            wait(fr.at[k, :, 1 - D, rows], f_recv.at[q, 4])

    def s1(q):
        k, pair_first, rows, _, _ = split(q)
        own = g2.at[k, y, A, c, rows]
        if q == 8 * SUB:
            wait(g2.at[pl.ds(8, 8), y, A, c], a_recv.at[0])
        push(own, own, g_send.at[q], g_recv.at[q, 4], a_pair)
        if not pair_first:
            push(own, own, g_send.at[q], g_recv.at[q, 0], y_up)
            push(own, own, g_send.at[q], g_recv.at[q, 1], y_down)

    def s2(q):
        k, pair_first, rows, lo, hi = split(q)
        if pair_first:
            wait(g2.at[k, y, 1 - A, c, rows], g_recv.at[q, 4])
            own = g2.at[k, y, :, c, rows]
            push(own, own, g_send.at[q], g_recv.at[q, 0], y_up)
            push(own, own, g_send.at[q], g_recv.at[q, 1], y_down)
        else:
            b = g2.at[k, y3, A, c]
            wait(b.at[rows], g_recv.at[q, 0])
            push(b.at[lo], b.at[lo], g_send.at[q], g_recv.at[q, 2], y_up)
            push(b.at[rows], b.at[rows], g_send.at[q], g_recv.at[q, 4], a_pair)
            b = g2.at[k, y1, A, c]
            wait(b.at[rows], g_recv.at[q, 1])
            push(b.at[hi], b.at[hi], g_send.at[q], g_recv.at[q, 3], y_down)
            push(b.at[rows], b.at[rows], g_send.at[q], g_recv.at[q, 4], a_pair)

    def s3(q):
        k, pair_first, rows, lo, hi = split(q)
        if pair_first:
            b = g2.at[k, y3, 0, c, rows]
            wait(g2.at[k, y3, :, c, rows], g_recv.at[q, 0])
            push(b, b, g_send.at[q], g_recv.at[q, 2], y_up)
            b = g2.at[k, y1, 1, c, rows]
            wait(g2.at[k, y1, :, c, rows], g_recv.at[q, 1])
            push(b, b, g_send.at[q], g_recv.at[q, 3], y_down)
        else:
            b = g2.at[k, y2, A, c]
            wait(b.at[lo], g_recv.at[q, 2])
            wait(b.at[hi], g_recv.at[q, 3])
            push(b.at[rows], b.at[rows], g_send.at[q], g_recv.at[q, 4], a_pair)

    def s4(q):
        k, pair_first, rows, lo, hi = split(q)
        if pair_first:
            wait(g2.at[k, y2, 0, c, rows], g_recv.at[q, 2])
            wait(g2.at[k, y2, 1, c, rows], g_recv.at[q, 3])
        else:
            wait(g2.at[k, :, 1 - A, c, rows], g_recv.at[q, 4])
        mine = g2.at[k, :, :, c, rows]
        push(mine, mine, g_send.at[q], g_recv.at[q, 5], sibling)
        finish(lambda: wait(units(15), g_send.at[q]))

    def s5(q):
        k, _, rows, _, _ = split(q)
        wait(g2.at[k, :, :, 1 - c, rows], g_recv.at[q, 5])

    def halfway(i):
        for q in range(2):
            acc = jnp.zeros((512, 256), F32)
            for m in range(8):
                rows = fr[pl.ds(4 * q, 4), m // 2, m % 2].reshape(512, 256)
                acc += jnp.dot(rows, g2[8 + i, m // 2, m % 2].reshape(256, 256), preferred_element_type=F32)
            half[pl.ds(4 * q, 4), pl.ds((i % 2) * 128, 128)] = acc.astype(BF16).reshape(4, 128, 256)

    def ladder(j, q):
        acc = jnp.zeros((256, 1024), F32)
        for p in range(8):
            acc += lax.dot_general(half[p], g2[p, pl.ds(2 * q, 2)].reshape(1024, 256), TRANSPOSED, preferred_element_type=F32)
        for h in range(2):
            for m in range(4):
                block = acc[h * 128:(h + 1) * 128, m * 256:(m + 1) * 256]
                part32[2 * j + h, 2 * q + m // 2, m % 2] = block
                part[2 * j + h, 2 * q + m // 2, m % 2] = block.astype(BF16)

    add = lambda *terms: functools.reduce(lambda a, b: a + b, [t.astype(F32) for t in terms])

    def owner_push(q, src_of, dst, sem):
        for cc in range(2):
            here = jnp.logical_and(on_home_chip, c == cc)
            src = src_of(cc)
            push_or_copy(here, src, dst, q_send.at[q, cc], sem, dev(y, 2 * A + c, z, cc))
            finish(lambda src=src, cc=cc, here=here: pl.when(jnp.logical_not(here))(lambda: wait(src, q_send.at[q, cc])))

    def scatter_first(i, q, block, first, second, two):
        send, rin = o_send.at[q], ring_in.at[i]
        push(block(z2, 0, first), rin.at[0, first], send, o_recv.at[q, 0], z_up)
        push(block(z2, 1, second), rin.at[two, second], send, o_recv.at[q, 1], z_down)
        push(block(z3, 0, first), rin.at[1, first], send, o_recv.at[q, 2], z_down)
        push(block(z1, 1, second), rin.at[two + 1, second], send, o_recv.at[q, 3], z_up)

    def o1(q):
        i, ring_first, rows, lo, hi = split(q)
        if ring_first:
            scatter_first(i, q, lambda zz, d, r: part.at[i, zz, d, r], rows, rows, 3)
        else:
            owner_push(q, lambda cc: part.at[i, :, cc, rows], pin.at[i, D, :, rows], o_recv.at[q, 4])

    def o2(q):
        i, ring_first, rows, lo, hi = split(q)
        rin = ring_in.at[i]
        if ring_first:
            wait(rin.at[0, rows], o_recv.at[q, 0])
            comb[i, 0, rows] = add(part32[i, z1, 0, rows], ring_in[i, 0, rows]).astype(BF16)
            push(comb.at[i, 0, rows], rin.at[2, rows], o_send.at[q], o_recv.at[q, 2], z_up)
            wait(rin.at[3, rows], o_recv.at[q, 1])
            comb[i, 1, rows] = add(part32[i, z3, 1, rows], ring_in[i, 3, rows]).astype(BF16)
            push(comb.at[i, 1, rows], rin.at[5, rows], o_send.at[q], o_recv.at[q, 3], z_down)
        else:
            wait(pin.at[i, :, :, rows], o_recv.at[q, 4])
            pp[i, :, rows] = add(pin[i, 0, :, rows], pin[i, 1, :, rows]).astype(BF16)
            scatter_first(i, q, lambda zz, d, r: pp.at[i, zz, r], lo, hi, 0)

    def o3(q):
        i, ring_first, rows, lo, hi = split(q)
        rin = ring_in.at[i]
        if ring_first:
            wait(rin.at[pl.ds(1, 2), rows], o_recv.at[q, 2])
            wait(rin.at[pl.ds(4, 2), rows], o_recv.at[q, 3])
            quad[i, 0, rows] = add(part32[i, z, 0, rows], ring_in[i, 1, rows], ring_in[i, 2, rows]).astype(BF16)
            quad[i, 1, rows] = add(part32[i, z, 1, rows], ring_in[i, 4, rows], ring_in[i, 5, rows]).astype(BF16)
            owner_push(q, lambda cc: quad.at[i, cc, rows], fin.at[i, D, rows], o_recv.at[q, 4])
            finish(lambda: wait(units(6), o_send.at[q]))
        else:
            wait(rin.at[0, lo], o_recv.at[q, 0])
            comb[i, 0, lo] = add(pin[i, 0, z1, lo], pin[i, 1, z1, lo], ring_in[i, 0, lo]).astype(BF16)
            push(comb.at[i, 0, lo], rin.at[2, lo], o_send.at[q], o_recv.at[q, 2], z_up)
            wait(rin.at[0, hi], o_recv.at[q, 1])
            comb[i, 0, hi] = add(pin[i, 0, z3, hi], pin[i, 1, z3, hi], ring_in[i, 0, hi]).astype(BF16)
            push(comb.at[i, 0, hi], rin.at[2, hi], o_send.at[q], o_recv.at[q, 3], z_down)
            finish(lambda: wait(units(3), o_send.at[q]))

    def o4(q):
        i, ring_first, rows, lo, hi = split(q)
        if ring_first:
            wait(fin.at[i, :, rows], o_recv.at[q, 4])
            out_ref[i, rows] = add(fin[i, 0, rows], fin[i, 1, rows])
        else:
            rin = ring_in.at[i]
            wait(rin.at[pl.ds(1, 2), lo], o_recv.at[q, 2])
            wait(rin.at[pl.ds(1, 2), hi], o_recv.at[q, 3])
            out_ref[i, rows] = add(pin[i, 0, z, rows], pin[i, 1, z, rows], ring_in[i, 1, rows], ring_in[i, 2, rows])

    at(SHARE_AT, -1, share_amplitudes)
    for q in range(8 * SUB):
        at(q - AHEAD, -1, e1, q)
        for s, step in enumerate((f1, f2, f3, f4)):
            at(q + s * FACTOR_LAG, s, step, q)
    for q in range(16 * SUB):
        lag = FACTOR_LAG if q < 8 * SUB else AMP_LAG
        for s, step in enumerate((s1, s2, s3, s4)):
            at(q + s * lag, 4 + s, step, q)
        at(q + 3 * lag + CORE_LAG, 8, s5, q)
    for j in range(4):
        ready = (8 + 2 * j) * SUB + 3 * AMP_LAG + CORE_LAG + READY
        at(ready + 1 * SUB - 1, 10, halfway, 2 * j)
        at(ready + 2 * SUB - 1, 10, halfway, 2 * j + 1)
        at(ready + 2 * SUB, 10, ladder, j, 0)
        at(ready + 2 * SUB + 1, 10, ladder, j, 1)
        for q in range(2 * j * SUB, 2 * (j + 1) * SUB):
            for s, step in enumerate((o1, o2, o3, o4)):
                at(ready + 2 * SUB + 1 + OUT_LAG * s, 11 + s, step, q)
    while plan:
        now[0], _, _, step, args = heapq.heappop(plan)
        step(*args)


def shards(amplitudes, df_factor, amp_mask, factor_mask):
    vmem, smem = pl.BlockSpec(memory_space=pltpu.VMEM), pl.BlockSpec(memory_space=pltpu.SMEM)
    block = lambda *lead: pltpu.VMEM((*lead, 128, 256), BF16)
    dma = lambda *shape: pltpu.SemaphoreType.DMA(shape)
    return pl.pallas_call(
        kernel,
        out_shape=jax.ShapeDtypeStruct((8, 128, 256), F32),
        in_specs=[vmem, vmem, smem, smem],
        out_specs=vmem,
        scratch_shapes=[
            pltpu.VMEM((8, 16, 2048), BF16),
            block(8),
            block(16, 4, 2, 2),
            block(8, 4, 2),
            pltpu.VMEM((8, 256, 256), BF16),
            block(8, 4, 2),
            pltpu.VMEM((8, 4, 2, 128, 256), F32),
            block(8, 6),
            block(8, 2),
            block(8, 2),
            block(8, 2),
            block(8, 2, 4),
            block(8, 4),
            dma(16 * SUB, 6), dma(16 * SUB), dma(8 * SUB, 6), dma(8 * SUB), dma(8 * SUB, 2), dma(1), dma(4, 2),
            dma(8 * SUB, 5), dma(8 * SUB), dma(8 * SUB, 2),
        ],
        compiler_params=pltpu.CompilerParams(collective_id=0, has_side_effects=True, vmem_limit_bytes=60 * 2**20),
        cost_estimate=pl.CostEstimate(flops=17179869184, bytes_accessed=4 * 2**20, transcendentals=0),
    )(amplitudes, df_factor, amp_mask, factor_mask)


def solution(mesh):
    return jax.shard_map(
        shards,
        mesh=mesh,
        in_specs=(P(None, ("wide", "narrow"), None), P(None, "wide", "narrow"), P(), P()),
        out_specs=P(None, "wide", "narrow"),
        check_vma=False,
    )
```

time: 319 us -> 112 us (0.35)
  waiting for transfers between devices: 224 us -> 0 us
  Pallas kernels: 0 us -> 110 us
  local copies, waits for them, and re-layouts: 36 us -> 2.27 us
  matrix products: 28.9 us -> 0 us
  between operations: 13.2 us -> 0.01 us
  other arithmetic: 9.36 us -> 0 us
  starting transfers between devices: 5.82 us -> 0 us
    pallas_call x0 -> x1, Pallas kernels: none -> 110 us  [shards(): pl.pallas_call(kernel, out_shape=jax.ShapeDtypeStruct((8, 128, 256), F32)...]
    all_to_all x1 -> x0, waiting for transfers between devices: 103 us -> none  [shards(): lax.all_to_all(collected, 'narrow', split_axis=2, concat_axis=1, tiled=True)]
    all_gather x3 -> x0, waiting for transfers between devices: 70.6 us -> none  [the longest x1 70.6 us: shards(): collected = lax.all_gather(amplitudes, 'wide', axis=1, tiled=True)]
    reduce_scatter x1 -> x0, waiting for transfers between devices: 50.1 us -> none  [shards(): lax.psum_scatter(partial_sums, 'narrow', scatter_dimension=2, tiled=True)]
    dot_general x5 -> x0, matrix products: 28.9 us -> none  [the longest x1 25.6 us: shards(): jnp.einsum('ipad,pbd->iab', halfway, lax.all_gather(factor, 'wide', axis=...]
    all_gather x1 -> x0, local copies, waits for them, and re-layouts: 13.4 us -> none  [shards(): collected = lax.all_gather(amplitudes, 'wide', axis=1, tiled=True)]
    all_to_all x1 -> x0, local copies, waits for them, and re-layouts: 12.6 us -> none  [shards(): lax.all_to_all(collected, 'narrow', split_axis=2, concat_axis=1, tiled=True)]
    mul x2 -> x0, other arithmetic: 9.33 us -> none  [the longest x1 7.45 us: shards(): amps = relaid * amp_table.astype(jnp.bfloat16)[None]]
  transfers between devices with their start and end apart: 5 -> 0, of which waited for: 3 -> 0; matrix products, arithmetic and copies ran while one was open for 15% -> 0% of each run, Pallas kernels for 0% -> 0%
where the time goes in v2:
time: 112 us
  Pallas kernels  110 us (98%)
  local copies, waits for them, and re-layouts  2.27 us (2%)
    pallas_call x1, Pallas kernels, shards(): pl.pallas_call(kernel, out_shape=jax.ShapeDtypeStruct((8, 128, 256), F32)...  110 us
    unnamed x1, local copies, waits for them, and re-layouts  2.27 us

profile of v2, /device:TPU:1, one launch (start us, length us, event | category | flops | bytes accessed | tf_op | source)
XLA Modules:
  0.0 112.3 jit_solution(17658947324122448771)
XLA Ops:
  0.0 110.0 %shard_map.46 = f32[8,128,256]{2,1,0:T(8,128)} custom-call(bf16[8,16,2048]{2,1,0:T(8,128)(2,1)} %amp_ref.1, bf16[8,128,256]{2,1,0:T(8,128)(2,1)} %fac_ref.1, s32[16,16]{1,0:T(8,128)} %amask.1, s32[16,16]{1,0:T(8,128)} %fmask.1), custom_call_target="tpu_custom_call" | custom-call | flops 17179869184 | bytes 4194304 | tf_op jit(solution)/shard_map/pallas_call | solution.py:345
  110.0 2.3 %copy.6 = f32[8,128,256]{2,1,0:T(8,128)} copy(f32[8,128,256]{2,1,0:T(8,128)} %shard_map.46) | data formatting | bytes 2097152

commit v3 on v0

v3 whole, which is shorter than its diff:
```python
import functools
import heapq

import jax
import jax.numpy as jnp
from jax import lax
from jax.experimental import pallas as pl
from jax.experimental.pallas import tpu as pltpu
from jax.sharding import PartitionSpec as P

MESH = pl.DeviceIdType.MESH
BF16 = jnp.bfloat16
F32 = jnp.float32
TRANSPOSED = (((1,), (1,)), ((), ()))

SUB = 2
ROWS = 128 // SUB
FACTOR_LAG = 3.0
AMP_LAG = 3.0
CORE_LAG = 1.0
OUT_LAG = 4.0
AHEAD = 6
SHARE_AT = 0.0
END_LAG = 8.0
RING_FIRST = (1, 3, 5, 7)
ROW_RING_FIRST = (1, 4, 6)
ROW_STEP = 2.25
ROW_LAG = 3.5
SECOND_HOP = 10.0
ORDER = (0, 1, 2, 3, 4, 5, 6, 7, 8, 9, 10, 11, 12, 13, 14, 15)
GROUPS = ((0, 1), (2, 3), (4, 5), (6,), (7,))


def kernel(amp_ref, fac_ref, amask, fmask, out_ref, tsrc, tmid, fsrc, g2, fr, half, part, part32, ring_in, comb, quad, fin, pin, pp,
           g_recv, g_send, core_recv, f_recv, f_all, f_send, e_send, a_recv, a_send, o_recv, o_send, q_send):
    w, n = lax.axis_index("wide"), lax.axis_index("narrow")
    y, x = w // 4, w % 4
    z, c = n // 2, n % 2
    A, xl = x // 2, x % 2
    D = ((x + 1) // 2) % 2
    up = lambda v, s: lax.rem(v + s + 4, 4)
    x_of = lambda a, d: a * 3 + d * (1 - 2 * a)
    dev = lambda yy, xx, zz, cc: (yy * 4 + xx, zz * 2 + cc)
    z1, z2, z3 = up(z, 1), up(z, 2), up(z, 3)
    y1, y2, y3 = up(y, 1), up(y, 2), up(y, 3)
    z_up, z_down = dev(y, x, z1, c), dev(y, x, z3, c)
    y_up, y_down = dev(y1, x, z, c), dev(y3, x, z, c)
    a_pair = dev(y, x_of(1 - A, D), z, c)
    d_pair = dev(y, x_of(A, 1 - D), z, c)
    sibling = dev(y, x, z, 1 - c)
    on_home_chip = x == 2 * A + c

    def push(src, dst, send, recv, to):
        pltpu.make_async_remote_copy(src_ref=src, dst_ref=dst, send_sem=send, recv_sem=recv, device_id=to, device_id_type=MESH).start()

    def push_or_copy(here, src, dst, send, recv, to):
        @pl.when(here)
        def _():
            pltpu.make_async_copy(src, dst, recv).start()

        @pl.when(jnp.logical_not(here))
        def _():
            push(src, dst, send, recv, to)

    def wait(ref, sem):
        pltpu.make_async_copy(ref, ref, sem).wait()

    def units(count, rows=ROWS):
        sizes = [(a, b, d, e) for a in range(1, 17) for b in range(1, 5) for d in (1, 2) for e in (1, 2) if a * b * d * e == count]
        a, b, d, e = sizes[0]
        return g2.at[pl.ds(0, a), pl.ds(0, b), pl.ds(0, d), pl.ds(0, e), pl.ds(0, rows)]

    def split(k, h, tall):
        first = h * tall
        pair_first = (k % 8 not in RING_FIRST) if tall == 128 else (h == 0 or k % 8 == 7)
        return pair_first, pl.ds(first, tall), pl.ds(first, tall // 2), pl.ds(first + tall // 2, tall // 2)

    barrier = pltpu.get_barrier_semaphore()
    for to in (sibling, d_pair, dev(y, x_of(A, 1 - D), z, 1 - c), z_up, z_down, dev(y, x, z2, c), y_up, y_down, a_pair):
        pl.semaphore_signal(barrier, inc=1, device_id=to, device_id_type=MESH)

    for h in range(2):
        keep = fmask[w, 2 * n + h].astype(F32)
        cols = pl.ds(h * 128, 128)
        fsrc[:, :, cols] = (fac_ref[:, :, cols].astype(F32) * keep).astype(BF16)
    for h in range(16):
        keep = amask[w, h].astype(F32)
        cols = pl.ds(h * 128, 128)
        tsrc[h // 4, (h // 2) % 2, :, :, pl.ds((h % 2) * 128, 128)] = (amp_ref[:, :, cols].astype(F32) * keep).astype(BF16)

    pl.semaphore_wait(barrier, 9)

    plan = []
    now = [-100.0, 0]

    def at(when, order, step, *args):
        now[1] += 1
        heapq.heappush(plan, (when, order, now[1], step, args))

    def finish(step):
        at(now[0] + END_LAG, 30, step)

    stays = [jnp.logical_and(x_of(A, d) == x, xl == c) for d in range(2)]

    def e1(k):
        for d in range(2):
            def go(d=d):
                push_or_copy(stays[d], fsrc.at[k], fr.at[k, z, c], e_send.at[d], f_recv.at[k, 0], dev(y, x_of(A, d), z, xl))

            if k in ROW_RING_FIRST:
                pl.when(c == d)(go)
            else:
                go()

    def e_end():
        for d in range(2):
            goes = jnp.logical_not(stays[d])
            pl.when(jnp.logical_and(goes, c == d))(lambda: wait(fsrc, e_send.at[d]))
            pl.when(jnp.logical_and(goes, c != d))(lambda: wait(fsrc.at[pl.ds(0, 8 - len(ROW_RING_FIRST))], e_send.at[d]))

    def t1():
        for d in range(2):
            dst = tmid.at[:, :, pl.ds(pl.multiple_of(c * 16, 16), 16)]
            push_or_copy(stays[d], tsrc.at[:, d], dst, a_send.at[d], a_recv.at[0], dev(y, x_of(A, d), z, xl))
            finish(lambda d=d: pl.when(jnp.logical_not(stays[d]))(lambda: wait(tsrc.at[:, d], a_send.at[d])))

    def t2():
        wait(tmid, a_recv.at[0])
        dst = g2.at[pl.ds(8, 8), y, A, c, pl.ds(pl.multiple_of(z * 32, 32), 32)]
        for zz in (z2, z1, z3):
            push(tmid.at[zz], dst, a_send.at[2], a_recv.at[1], dev(y, x, zz, c))
        pltpu.make_async_copy(tmid.at[z], dst, a_recv.at[1]).start()
        finish(lambda: wait(tmid.at[pl.ds(0, 3)], a_send.at[2]))

    def t3():
        wait(g2.at[pl.ds(8, 8), y, A, c], a_recv.at[1])

    def f0(k):
        wait(fr.at[k, z] if k not in ROW_RING_FIRST else fr.at[k, z, D], f_recv.at[k, 0])
        g2[k, y, A, c] = fr[k, z, D]

    def f1(k):
        pair_first = k not in ROW_RING_FIRST
        own = fr.at[k, z] if pair_first else fr.at[k, z, D]
        push(own, own, f_send.at[k], f_recv.at[k, 1], z_up)
        push(own, own, f_send.at[k], f_recv.at[k, 1], z_down)
        if not pair_first:
            push(own, own, f_send.at[k], f_all.at[0], d_pair)

    def f2(k):
        pair_first, lo, hi = k not in ROW_RING_FIRST, pl.ds(0, 64), pl.ds(64, 64)
        wait(units(4 if pair_first else 2, 128), f_recv.at[k, 1])
        if pair_first:
            push(fr.at[k, z3, 0], fr.at[k, z3, 0], f_send.at[k], f_all.at[0], z_up)
            push(fr.at[k, z1, 1], fr.at[k, z1, 1], f_send.at[k], f_all.at[0], z_down)
        else:
            push(fr.at[k, z3, D, lo], fr.at[k, z3, D, lo], f_send.at[k], f_recv.at[k, 2], z_up)
            push(fr.at[k, z1, D, hi], fr.at[k, z1, D, hi], f_send.at[k], f_recv.at[k, 2], z_down)
            push(fr.at[k, z3, D], fr.at[k, z3, D], f_send.at[k], f_all.at[0], d_pair)
            push(fr.at[k, z1, D], fr.at[k, z1, D], f_send.at[k], f_all.at[0], d_pair)

    def f3(k):
        pair_first, lo, hi = k not in ROW_RING_FIRST, pl.ds(0, 64), pl.ds(64, 64)
        if not pair_first:
            wait(fr.at[k, z2, D], f_recv.at[k, 2])
            push(fr.at[k, z2, D], fr.at[k, z2, D], f_send.at[k], f_all.at[0], d_pair)
        finish(lambda: wait(units(6 if pair_first else 7, 128), f_send.at[k]))

    def f4():
        wait(units(2 * (8 - len(ROW_RING_FIRST)) + 4 * len(ROW_RING_FIRST), 128), f_all.at[0])

    def s1(k, h, tall, at_sem):
        pair_first, rows, _, _ = split(k, h, tall)
        own = g2.at[k, y, A, c, rows]
        push(own, own, g_send.at[at_sem], g_recv.at[at_sem, 2], a_pair)
        if not pair_first:
            push(own, own, g_send.at[at_sem], g_recv.at[at_sem, 0], y_up)
            push(own, own, g_send.at[at_sem], g_recv.at[at_sem, 0], y_down)

    def s2(k, h, tall, at_sem):
        pair_first, rows, lo, hi = split(k, h, tall)
        send, recv = g_send.at[at_sem], g_recv.at[at_sem]
        if pair_first:
            wait(g2.at[k, y, 1 - A, c, rows], recv.at[2])
            own = g2.at[k, y, :, c, rows]
            push(own, own, send, recv.at[0], y_up)
            push(own, own, send, recv.at[0], y_down)
        else:
            wait(units(2, tall), recv.at[0])
            b, d = g2.at[k, y3, A, c], g2.at[k, y1, A, c]
            push(b.at[lo], b.at[lo], send, recv.at[1], y_up)
            push(d.at[hi], d.at[hi], send, recv.at[1], y_down)
            push(b.at[rows], b.at[rows], send, recv.at[2], a_pair)
            push(d.at[rows], d.at[rows], send, recv.at[2], a_pair)

    def s3(k, h, tall, at_sem):
        pair_first, rows, lo, hi = split(k, h, tall)
        send, recv = g_send.at[at_sem], g_recv.at[at_sem]
        if pair_first:
            wait(units(4, tall), recv.at[0])
            b, d = g2.at[k, y3, 0, c, rows], g2.at[k, y1, 1, c, rows]
            push(b, b, send, recv.at[1], y_up)
            push(d, d, send, recv.at[1], y_down)
        else:
            b = g2.at[k, y2, A, c, rows]
            wait(b, recv.at[1])
            push(b, b, send, recv.at[2], a_pair)

    def s4(k, h, tall, at_sem):
        pair_first, rows, lo, hi = split(k, h, tall)
        if pair_first:
            wait(g2.at[k, y2, :, c, rows], g_recv.at[at_sem, 1])
        else:
            wait(g2.at[k, :, 1 - A, c, rows], g_recv.at[at_sem, 2])
        mine = g2.at[k, :, :, c, rows]
        push(mine, mine, g_send.at[at_sem], core_recv.at[0 if k < 8 else k - 7], sibling)
        finish(lambda: wait(units(15, tall), g_send.at[at_sem]))

    def columns_in():
        wait(g2.at[pl.ds(0, 8), :, :, 1 - c], core_recv.at[0])

    def amps_in(k):
        wait(g2.at[k, :, :, 1 - c], core_recv.at[k - 7])

    def halfway(i, slot):
        for q in range(2):
            acc = jnp.zeros((512, 256), F32)
            for m in range(8):
                rows = fr[pl.ds(4 * q, 4), m // 2, m % 2].reshape(512, 256)
                acc += jnp.dot(rows, g2[8 + i, m // 2, m % 2].reshape(256, 256), preferred_element_type=F32)
            half[pl.ds(4 * q, 4), pl.ds(slot * 128, 128)] = acc.astype(BF16).reshape(4, 128, 256)

    def ladder(group, q):
        tall = pl.ds(0, 128 * len(group))
        acc = jnp.zeros((128 * len(group), 1024), F32)
        for p in range(8):
            acc += lax.dot_general(half[p, tall], g2[p, pl.ds(2 * q, 2)].reshape(1024, 256), TRANSPOSED, preferred_element_type=F32)
        for h, i in enumerate(group):
            for m in range(4):
                block = acc[h * 128:(h + 1) * 128, m * 256:(m + 1) * 256]
                part32[i, 2 * q + m // 2, m % 2] = block
                part[i, 2 * q + m // 2, m % 2] = block.astype(BF16)

    add = lambda *terms: functools.reduce(lambda a, b: a + b, [t.astype(F32) for t in terms])

    owns = [jnp.logical_and(on_home_chip, c == cc) for cc in range(2)]

    def owner_push(src_of, dst, send, sem):
        for cc in range(2):
            push_or_copy(owns[cc], src_of(cc), dst, q_send.at[send, cc], sem, dev(y, 2 * A + c, z, cc))

    def q_end():
        for cc in range(2):
            for send, count in enumerate(sent):
                pl.when(jnp.logical_not(owns[cc]))(lambda: wait(units(count), q_send.at[send, cc]))

    sent = [0, 0]

    def scatter_first(i, q, block, first, second, two):
        send, rin = o_send.at[q], ring_in.at[i]
        push(block(z2, 0, first), rin.at[0, first], send, o_recv.at[q, 0], z_up)
        push(block(z2, 1, second), rin.at[two, second], send, o_recv.at[q, 0], z_down)
        push(block(z3, 0, first), rin.at[1, first], send, o_recv.at[q, 1], z_down)
        push(block(z1, 1, second), rin.at[two + 1, second], send, o_recv.at[q, 1], z_up)

    def o1(i, h):
        ring_first, rows, lo, hi = split(i, h, ROWS)
        q = i * SUB + h
        if ring_first:
            scatter_first(i, q, lambda zz, d, r: part.at[i, zz, d, r], rows, rows, 3)
        else:
            owner_push(lambda cc: part.at[i, :, cc, rows], pin.at[i, D, :, rows], 1, o_recv.at[q, 2])
            sent[1] += 4

    def o2(i, h):
        ring_first, rows, lo, hi = split(i, h, ROWS)
        q = i * SUB + h
        rin = ring_in.at[i]
        if ring_first:
            wait(units(2), o_recv.at[q, 0])
            comb[i, 0, rows] = add(part32[i, z1, 0, rows], ring_in[i, 0, rows]).astype(BF16)
            push(comb.at[i, 0, rows], rin.at[2, rows], o_send.at[q], o_recv.at[q, 1], z_up)
            comb[i, 1, rows] = add(part32[i, z3, 1, rows], ring_in[i, 3, rows]).astype(BF16)
            push(comb.at[i, 1, rows], rin.at[5, rows], o_send.at[q], o_recv.at[q, 1], z_down)
        else:
            wait(pin.at[i, :, :, rows], o_recv.at[q, 2])
            pp[i, :, rows] = add(pin[i, 0, :, rows], pin[i, 1, :, rows]).astype(BF16)
            scatter_first(i, q, lambda zz, d, r: pp.at[i, zz, r], lo, hi, 0)

    def o3(i, h):
        ring_first, rows, lo, hi = split(i, h, ROWS)
        q = i * SUB + h
        rin = ring_in.at[i]
        if ring_first:
            wait(units(4), o_recv.at[q, 1])
            quad[i, 0, rows] = add(part32[i, z, 0, rows], ring_in[i, 1, rows], ring_in[i, 2, rows]).astype(BF16)
            quad[i, 1, rows] = add(part32[i, z, 1, rows], ring_in[i, 4, rows], ring_in[i, 5, rows]).astype(BF16)
            owner_push(lambda cc: quad.at[i, cc, rows], fin.at[i, D, rows], 0, o_recv.at[q, 2])
            sent[0] += 1
            finish(lambda: wait(units(6), o_send.at[q]))
        else:
            wait(rin.at[0, rows], o_recv.at[q, 0])
            comb[i, 0, lo] = add(pin[i, 0, z1, lo], pin[i, 1, z1, lo], ring_in[i, 0, lo]).astype(BF16)
            push(comb.at[i, 0, lo], rin.at[2, lo], o_send.at[q], o_recv.at[q, 1], z_up)
            comb[i, 0, hi] = add(pin[i, 0, z3, hi], pin[i, 1, z3, hi], ring_in[i, 0, hi]).astype(BF16)
            push(comb.at[i, 0, hi], rin.at[2, hi], o_send.at[q], o_recv.at[q, 1], z_down)
            finish(lambda: wait(units(3), o_send.at[q]))

    def o4(i, h):
        ring_first, rows, lo, hi = split(i, h, ROWS)
        q = i * SUB + h
        if ring_first:
            wait(fin.at[i, :, rows], o_recv.at[q, 2])
            out_ref[i, rows] = add(fin[i, 0, rows], fin[i, 1, rows])
        else:
            wait(units(2), o_recv.at[q, 1])
            out_ref[i, rows] = add(pin[i, 0, z, rows], pin[i, 1, z, rows], ring_in[i, 1, rows], ring_in[i, 2, rows])

    at(SHARE_AT, -1, t1)
    at(SECOND_HOP, -1, t2)
    for k in range(8):
        at(k * SUB - AHEAD, -2, e1, k)
        at(k * SUB, -1, f0, k)
        for s, step in enumerate((f1, f2, f3)):
            at(k * ROW_STEP + s * ROW_LAG, s, step, k)
    rows_done = 7 * ROW_STEP + 2 * ROW_LAG + 2
    at(rows_done, 9, f4)
    at(8 * SUB, 31, e_end)
    done = {}
    amps_at = None
    for place, k in enumerate(ORDER):
        lag, parts = (FACTOR_LAG, 1) if k < 8 else (AMP_LAG, SUB)
        if k >= 8 and amps_at is None:
            amps_at = place * SUB
            at(amps_at, 3, t3)
        for h in range(parts):
            start = place * SUB + h
            for s, step in enumerate((s1, s2, s3, s4)):
                at(start + s * lag, 4 + s, step, k, h, 128 // parts, k if k < 8 else 8 + (k - 8) * SUB + h)
        done[k] = place * SUB + parts - 1 + 3 * lag + CORE_LAG
        if k >= 8:
            at(done[k], 8, amps_in, k)
    columns_done = max(done[k] for k in range(8))
    at(columns_done, 8, columns_in)
    last = 0
    for group in GROUPS:
        when = max(rows_done, last)
        for slot, i in enumerate(group):
            when = max(when, done[8 + i])
            at(when, 10, halfway, i, slot)
            when += 1
        when = max(when, columns_done)
        at(when, 10, ladder, group, 0)
        last = when + 1
        at(last, 10, ladder, group, 1)
        for i in group:
            for h in range(SUB):
                for s, step in enumerate((o1, o2, o3, o4)):
                    at(last + OUT_LAG * s, 11 + s, step, i, h)
    at(1000, 40, q_end)
    while plan:
        now[0], _, _, step, args = heapq.heappop(plan)
        step(*args)


def shards(amplitudes, df_factor, amp_mask, factor_mask):
    vmem, smem = pl.BlockSpec(memory_space=pltpu.VMEM), pl.BlockSpec(memory_space=pltpu.SMEM)
    block = lambda *lead: pltpu.VMEM((*lead, 128, 256), BF16)
    dma = lambda *shape: pltpu.SemaphoreType.DMA(shape)
    return pl.pallas_call(
        kernel,
        out_shape=jax.ShapeDtypeStruct((8, 128, 256), F32),
        in_specs=[vmem, vmem, smem, smem],
        out_specs=vmem,
        scratch_shapes=[
            pltpu.VMEM((4, 2, 8, 16, 256), BF16),
            pltpu.VMEM((4, 8, 32, 256), BF16),
            block(8),
            block(16, 4, 2, 2),
            block(8, 4, 2),
            pltpu.VMEM((8, 256, 256), BF16),
            block(8, 4, 2),
            pltpu.VMEM((8, 4, 2, 128, 256), F32),
            block(8, 6),
            block(8, 2),
            block(8, 2),
            block(8, 2),
            block(8, 2, 4),
            block(8, 4),
            dma(8 + 8 * SUB, 3), dma(8 + 8 * SUB), dma(9), dma(8, 3), dma(1), dma(8), dma(2), dma(2), dma(3),
            dma(8 * SUB, 3), dma(8 * SUB), dma(2, 2),
        ],
        compiler_params=pltpu.CompilerParams(collective_id=0, has_side_effects=True, vmem_limit_bytes=60 * 2**20),
        cost_estimate=pl.CostEstimate(flops=17179869184, bytes_accessed=4 * 2**20, transcendentals=0),
    )(amplitudes, df_factor, amp_mask, factor_mask)


def solution(mesh):
    return jax.shard_map(
        shards,
        mesh=mesh,
        in_specs=(P(None, ("wide", "narrow"), None), P(None, "wide", "narrow"), P(), P()),
        out_specs=P(None, "wide", "narrow"),
        check_vma=False,
    )
```

time: 319 us -> 110 us (0.34)
  waiting for transfers between devices: 224 us -> 0 us
  Pallas kernels: 0 us -> 108 us
  local copies, waits for them, and re-layouts: 36 us -> 2.27 us
  matrix products: 28.9 us -> 0 us
  between operations: 13.2 us -> 0.01 us
  other arithmetic: 9.36 us -> 0 us
  starting transfers between devices: 5.82 us -> 0 us
    pallas_call x0 -> x1, Pallas kernels: none -> 108 us  [shards(): pl.pallas_call(kernel, out_shape=jax.ShapeDtypeStruct((8, 128, 256), F32)...]
    all_to_all x1 -> x0, waiting for transfers between devices: 103 us -> none  [shards(): lax.all_to_all(collected, 'narrow', split_axis=2, concat_axis=1, tiled=True)]
    all_gather x3 -> x0, waiting for transfers between devices: 70.6 us -> none  [the longest x1 70.6 us: shards(): collected = lax.all_gather(amplitudes, 'wide', axis=1, tiled=True)]
    reduce_scatter x1 -> x0, waiting for transfers between devices: 50.1 us -> none  [shards(): lax.psum_scatter(partial_sums, 'narrow', scatter_dimension=2, tiled=True)]
    dot_general x5 -> x0, matrix products: 28.9 us -> none  [the longest x1 25.6 us: shards(): jnp.einsum('ipad,pbd->iab', halfway, lax.all_gather(factor, 'wide', axis=...]
    all_gather x1 -> x0, local copies, waits for them, and re-layouts: 13.4 us -> none  [shards(): collected = lax.all_gather(amplitudes, 'wide', axis=1, tiled=True)]
    all_to_all x1 -> x0, local copies, waits for them, and re-layouts: 12.6 us -> none  [shards(): lax.all_to_all(collected, 'narrow', split_axis=2, concat_axis=1, tiled=True)]
    mul x2 -> x0, other arithmetic: 9.33 us -> none  [the longest x1 7.45 us: shards(): amps = relaid * amp_table.astype(jnp.bfloat16)[None]]
  transfers between devices with their start and end apart: 5 -> 0, of which waited for: 3 -> 0; matrix products, arithmetic and copies ran while one was open for 15% -> 0% of each run, Pallas kernels for 0% -> 0%
where the time goes in v3:
time: 110 us
  Pallas kernels  108 us (98%)
  local copies, waits for them, and re-layouts  2.27 us (2%)
    pallas_call x1, Pallas kernels, shards(): pl.pallas_call(kernel, out_shape=jax.ShapeDtypeStruct((8, 128, 256), F32)...  108 us
    unnamed x1, local copies, waits for them, and re-layouts  2.27 us

profile of v3, /device:TPU:1, one launch (start us, length us, event | category | flops | bytes accessed | tf_op | source)
XLA Modules:
  0.0 110.1 jit_solution(15299457893572105584)
XLA Ops:
  0.0 107.9 %shard_map.46 = f32[8,128,256]{2,1,0:T(8,128)} custom-call(bf16[8,16,2048]{2,1,0:T(8,128)(2,1)} %amp_ref.1, bf16[8,128,256]{2,1,0:T(8,128)(2,1)} %fac_ref.1, s32[16,16]{1,0:T(8,128)} %amask.1, s32[16,16]{1,0:T(8,128)} %fmask.1), custom_call_target="tpu_custom_call" | custom-call | flops 17179869184 | bytes 4194304 | tf_op jit(solution)/shard_map/pallas_call | solution.py:370
  107.9 2.3 %copy.6 = f32[8,128,256]{2,1,0:T(8,128)} copy(f32[8,128,256]{2,1,0:T(8,128)} %shard_map.46) | data formatting | bytes 2097152

commit v4 on v3

--- a/solution.py
+++ b/solution.py
@@ -25,10 +25,10 @@
 RING_FIRST = (1, 3, 5, 7)
 ROW_RING_FIRST = (1, 4, 6)
 ROW_STEP = 2.25
-ROW_LAG = 3.5
+ROW_LAG = 5.0
 SECOND_HOP = 10.0
 ORDER = (0, 1, 2, 3, 4, 5, 6, 7, 8, 9, 10, 11, 12, 13, 14, 15)
-GROUPS = ((0, 1), (2, 3), (4, 5), (6,), (7,))
+GROUPS = ((0, 1), (2, 3), (4, 5), (6, 7))
 
 
 def kernel(amp_ref, fac_ref, amask, fmask, out_ref, tsrc, tmid, fsrc, g2, fr, half, part, part32, ring_in, comb, quad, fin, pin, pp,

time: 110 us -> 107 us (0.973)
  Pallas kernels: 108 us -> 104 us
    pallas_call x1, Pallas kernels: 108 us -> 104 us  [shards(): pl.pallas_call(kernel, out_shape=jax.ShapeDtypeStruct((8, 128, 256), F32)...]
where the time goes in v4:
time: 107 us; the launch traced here: 106 us
  Pallas kernels  104 us (97%)
  local copies, waits for them, and re-layouts  2.27 us (2%)
    pallas_call x1, Pallas kernels, shards(): pl.pallas_call(kernel, out_shape=jax.ShapeDtypeStruct((8, 128, 256), F32)...  104 us
    unnamed x1, local copies, waits for them, and re-layouts  2.27 us

profile of v4, /device:TPU:1, one launch (start us, length us, event | category | flops | bytes accessed | tf_op | source)
XLA Modules:
  0.0 106.4 jit_solution(7216359558559237669)
XLA Ops:
  0.0 104.1 %shard_map.46 = f32[8,128,256]{2,1,0:T(8,128)} custom-call(bf16[8,16,2048]{2,1,0:T(8,128)(2,1)} %amp_ref.1, bf16[8,128,256]{2,1,0:T(8,128)(2,1)} %fac_ref.1, s32[16,16]{1,0:T(8,128)} %amask.1, s32[16,16]{1,0:T(8,128)} %fmask.1), custom_call_target="tpu_custom_call" | custom-call | flops 17179869184 | bytes 4194304 | tf_op jit(solution)/shard_map/pallas_call | solution.py:370
  104.1 2.3 %copy.6 = f32[8,128,256]{2,1,0:T(8,128)} copy(f32[8,128,256]{2,1,0:T(8,128)} %shard_map.46) | data formatting | bytes 2097152

commit v5 on v4

--- a/solution.py
+++ b/solution.py
@@ -15,17 +15,17 @@
 
 SUB = 2
 ROWS = 128 // SUB
-FACTOR_LAG = 3.0
+FACTOR_LAG = 3.5
 AMP_LAG = 3.0
 CORE_LAG = 1.0
-OUT_LAG = 4.0
+OUT_LAG = 5.0
 AHEAD = 6
 SHARE_AT = 0.0
 END_LAG = 8.0
 RING_FIRST = (1, 3, 5, 7)
 ROW_RING_FIRST = (1, 4, 6)
-ROW_STEP = 2.25
-ROW_LAG = 5.0
+ROW_STEP = 2.0
+ROW_LAG = 6.0
 SECOND_HOP = 10.0
 ORDER = (0, 1, 2, 3, 4, 5, 6, 7, 8, 9, 10, 11, 12, 13, 14, 15)
 GROUPS = ((0, 1), (2, 3), (4, 5), (6, 7))

time: 107 us -> 106 us (level)
  no operation moved by 1% of the time
where the time goes in v5:
time: 106 us
  Pallas kernels  104 us (98%)
  local copies, waits for them, and re-layouts  2.27 us (2%)
    pallas_call x1, Pallas kernels, shards(): pl.pallas_call(kernel, out_shape=jax.ShapeDtypeStruct((8, 128, 256), F32)...  104 us
    unnamed x1, local copies, waits for them, and re-layouts  2.27 us

profile of v5, /device:TPU:1, one launch (start us, length us, event | category | flops | bytes accessed | tf_op | source)
XLA Modules:
  0.0 106.1 jit_solution(5760952572353659365)
XLA Ops:
  0.0 103.8 %shard_map.46 = f32[8,128,256]{2,1,0:T(8,128)} custom-call(bf16[8,16,2048]{2,1,0:T(8,128)(2,1)} %amp_ref.1, bf16[8,128,256]{2,1,0:T(8,128)(2,1)} %fac_ref.1, s32[16,16]{1,0:T(8,128)} %amask.1, s32[16,16]{1,0:T(8,128)} %fmask.1), custom_call_target="tpu_custom_call" | custom-call | flops 17179869184 | bytes 4194304 | tf_op jit(solution)/shard_map/pallas_call | solution.py:370
  103.8 2.3 %copy.6 = f32[8,128,256]{2,1,0:T(8,128)} copy(f32[8,128,256]{2,1,0:T(8,128)} %shard_map.46) | data formatting | bytes 2097152
